TPU v7x, 32 devices: a whole 2x2x4 slice. The times are simulated.
32 devices in a mesh: tp: 2 (over core), dp: 16 (over z, y, x).
Axes of the slice: x: 2, y: 2, z: 4, core: 2. Of those that a mesh axis runs over, the one named last changes fastest.
Arguments:
- hidden: bfloat16 [32768, 8192], P('dp', 'tp')
- norm_gain: bfloat16 [8192], P('tp'), may hold values from 0.099609375 to 1.8984375
- projection: bfloat16 [8192, 1024], P('tp'), may hold values from -0.0625 to 0.0625
- centroids: bfloat16 [65536, 1024], P('dp'), may hold values from -6 to 6
- owners: int32 [32768, 1], P(('dp', 'tp')), may hold values from 0 to 15; in each aligned block of 1024 rows (0 to 1023, 1024 to 2047, ...) at most 192 rows name the same one
- local_list: int32 [32768], P(('dp', 'tp')), may hold values from 0 to 4095
- slot_table: int32 [32, 3072], P(('dp', 'tp')), may hold values from 0 to 3071, each once within a row
Outputs:
- codes: bfloat16 [98304, 1024], P(('dp', 'tp'))
Inputs may be any that keep to these rules, and one draw needn't show every extreme that they name: `owners`: in the 1024 tokens of one device no owner is named more than 192 times; some device names an owner exactly 192 times. `slot_table`: each row is a permutation of 0 to 3071.
All inputs are finite; a program needn't handle non-finite values.
Results may differ from a plain program's by a relative error of at most 0.011.
Values may be sent and summed in bfloat16 or wider, within the bound.
No kernel may reach another device: no remote copies, remote signals or barrier semaphores. Data moves between devices by JAX's collectives and lax.ppermute only.
A program may use at most 128 MiB of HBM per device.

v0:
```python
import jax
import jax.numpy as jnp
from jax import lax
from jax.sharding import PartitionSpec as P

D = 8192


EPSILON = 1e-05


def shards(hidden, norm_gain, projection, centroids, owners, local_list, slot_table):
    n_dp = lax.axis_size("dp")
    values = hidden.astype(jnp.float32)
    energy = lax.psum(jnp.sum(values * values, axis=1), "tp")
    inv_rms = lax.rsqrt(energy / D + EPSILON)
    normed = (values * norm_gain.astype(jnp.float32)[None, :] * inv_rms[:, None]).astype(
        jnp.bfloat16
    )
    slot_cap = slot_table.shape[1] // n_dp
    key_width = projection.shape[1]
    owner_iota = jnp.arange(n_dp, dtype=jnp.int32)
    product = jnp.dot(normed, projection, preferred_element_type=jnp.float32)
    key_rows = lax.psum_scatter(
        lax.optimization_barrier(product.astype(jnp.bfloat16))
        .astype(jnp.float32)
        .astype(jnp.bfloat16),
        "tp",
        scatter_dimension=0,
        tiled=True,
    ).astype(jnp.float32)
    owner_ids = owners[:, 0]
    onehot = (owner_ids[:, None] == owner_iota[None, :]).astype(jnp.int32)
    running = jnp.cumsum(onehot, axis=0)
    rank_in = jnp.sum(onehot * (running - 1), axis=1)
    flat_pos = owner_ids * slot_cap + rank_in
    outgoing = jnp.zeros((n_dp * slot_cap, key_width), jnp.float32).at[flat_pos].set(key_rows)
    outgoing = outgoing.reshape(n_dp, slot_cap, key_width)
    list_ids = jnp.full((n_dp * slot_cap,), -1, jnp.int32).at[flat_pos].set(local_list)
    list_ids = list_ids.reshape(n_dp, slot_cap)
    arrived, arrived_lists = (
        lax.all_to_all(
            outgoing.astype(jnp.bfloat16), "dp", split_axis=0, concat_axis=0, tiled=True
        ).astype(outgoing.dtype),
        lax.all_to_all(list_ids, "dp", split_axis=0, concat_axis=0, tiled=True),
    )
    arrived = arrived.reshape(n_dp * slot_cap, key_width)
    arrived_lists = arrived_lists.reshape(n_dp * slot_cap)
    is_live = arrived_lists >= 0
    centre_rows = jnp.take(centroids, jnp.maximum(arrived_lists, 0), axis=0).astype(jnp.float32)
    residual = jnp.where(is_live[:, None], arrived - centre_rows, 0.0).astype(jnp.bfloat16)
    buffer = jnp.zeros((n_dp * slot_cap, key_width), jnp.bfloat16).at[slot_table[0]].set(residual)
    return buffer


def solution(mesh):
    placed = (
        P("dp", "tp"),
        P("tp"),
        P("tp", None),
        P("dp", None),
        P(("dp", "tp"), None),
        P(("dp", "tp")),
        P(("dp", "tp"), None),
    )
    return jax.shard_map(
        shards, mesh=mesh, in_specs=placed, out_specs=P(("dp", "tp"), None), check_vma=False
    )
```

profile of v0, /device:TPU:21, one launch (start us, length us, event | category | flops | bytes accessed | tf_op | source)
XLA Modules:
  0.0 356.3 jit_solution(17543701062384756494)
XLA Ops:
  6.5 7.2 %fusion.2 = f32[2048]{0:T(1024)S(1)} fusion(bf16[2048,4096]{1,0:T(8,128)(2,1)} %param.7), kind=kLoop, calls=%fused_computation.8 | loop fusion | flops 25163776 | bytes 16785408 | tf_op jit(solution)/shard_map/reduce_sum | solution.py:15
  13.8 2.8 psum.7
  16.6 0.0 copy-start
  16.6 24.1 %fusion.18 = bf16[2048,1024]{1,0:T(8,128)(2,1)} fusion(bf16[4096,1024]{1,0:T(8,128)(2,1)} %param.9, bf16[2048,4096]{1,0:T(8,128)(2,1)} %param.7, f32[2048]{0:T(1024)S(1)} %add_rsqrt_fusion, f32[4096]{0:T(1024)S(1)} %convert_element_type.37), kind=kOutput, calls=%fused_computation.23 | convolution fusion | flops 17215520768 | bytes 29384704 | tf_op jit(solution)/shard_map/dot_general | solution.py:23
  40.7 0.0 reduce-scatter.2.cloned.1.call-update
  40.8 4.5 %reduce-window.6 = s32[16,8,128]{2,1,0:T(8,128)S(1)} reduce-window(s32[16,8,128]{2,1,0:T(8,128)S(1)} %fusion.25, s32[]{:T(128)} %constant.15.clone.1), window={size=1x1x128 pad=0_0x0_0x127_0}, to_apply=%region_0.0 | reduce-window | flops 2080768 | bytes 131076 | tf_op jit(solution)/shard_map/reduce-window
  45.3 0.1 slice.10
  45.4 0.1 copy.12
  45.5 0.1 copy.13
  45.6 0.1 add_add_fusion
  45.8 4.5 %scatter_custom_fusion = s32[3072]{0:T(1024)S(1)} fusion(s32[1024]{0:T(1024)S(1)} %bitcast.32, s32[1024]{0:T(1024)} %param.12, s32[]{:T(128)} %constant.17.clone.1), kind=kCustom, calls=%fused_computation.40 | custom fusion | bytes 12800 | tf_op jit(solution)/shard_map/scatter | solution.py:39
  50.3 0.7 all_to_all.9
  50.9 6.5 %all-to-all-start = ((s32[16,1,192]{2,1,0:T(1,128)}), s32[16,1,192]{2,1,0:T(1,128)S(1)}, u32[]{:S(2)}, u32[]{:S(2)}) async-start(s32[16,1,192]{2,1,0:T(1,128)} %all_to_all.9), calls=%async_computation | async-start | bytes 32768 | tf_op jit(solution)/shard_map/all_to_all | solution.py:45
  57.4 0.0 reduce-scatter.2.cloned.1.call-done
  57.4 11.1 %scatter_custom_fusion.1 = f32[3072,1024]{1,0:T(8,128)} fusion(s32[1024]{0:T(1024)S(1)} %bitcast.33, f32[]{:T(128)} %constant.19.clone.1, bf16[1024,1024]{1,0:T(8,128)(2,1)} %reduce-scatter.2.cloned.1.call-done), kind=kCustom, calls=%fused_computation.18 | custom fusion | flops 1048576 | bytes 14680068 | tf_op jit(solution)/shard_map/scatter | solution.py:37
  68.5 8.3 %convert_element_type.41 = bf16[3072,1024]{1,0:T(8,128)(2,1)} convert(f32[3072,1024]{1,0:T(8,128)} %scatter_custom_fusion.1) | non-fusion elementwise | flops 3145728 | bytes 18874368 | tf_op jit(solution)/shard_map/convert_element_type | solution.py:43
  76.8 6.5 %all-to-all-start.1 = ((bf16[16,192,1024]{2,1,0:T(8,128)(2,1)}), bf16[16,192,1024]{2,1,0:T(8,128)(2,1)}, u32[]{:S(2)}, u32[]{:S(2)}) async-start(bf16[16,192,1024]{2,1,0:T(8,128)(2,1)} %bitcast.25), calls=%async_computation.2 | async-start | bytes 12582912 | tf_op jit(solution)/shard_map/all_to_all | solution.py:42
  83.3 0.1 compare_reduce_fusion.1
  83.4 0.1 le.16
  83.5 0.1 ge.18
  83.6 0.1 maximum_reduce_fusion
  83.7 0.1 reshape.101
  83.8 138.4 %all-to-all-done.1 = bf16[16,192,1024]{2,1,0:T(8,128)(2,1)} async-done(((bf16[16,192,1024]{2,1,0:T(8,128)(2,1)}), bf16[16,192,1024]{2,1,0:T(8,128)(2,1)}, u32[]{:S(2)}, u32[]{:S(2)}) %all-to-all-start.1) | async-done | bytes 6291488 | tf_op jit(solution)/shard_map/all_to_all | solution.py:42
  222.1 127.3 %scatter_custom_fusion.2 = bf16[3072,1024]{1,0:T(8,128)(2,1)} fusion(s32[3072]{0:T(1024)S(1)} %bitcast.31, bf16[3072,1024]{1,0:T(8,128)(2,1)} %bitcast.10, f32[]{:T(128)} %constant.19.clone.1, pred[3072]{0:T(1024)(128)(4,1)S(1)} %le.16, pred[3072]{0:T(1024)(128)(4,1)S(1)} %ge.18, bf16[]{:T(256)} %constant.42.clone.1, bf16[]{:T(256)} %constant.13.clone.1, ...), kind=kCustom, calls=%fused_computation.15 | custom fusion | flops 15728640 | bytes 20989960 | tf_op jit(solution)/shard_map/scatter | solution.py:52
  (16 shorter events, 0.1 us)
Async XLA Ops:
  6.5 10.1 %copy-start.2 = (bf16[4096]{0:T(1024)(128)(2,1)S(1)}, bf16[4096]{0:T(1024)(128)(2,1)}, u32[]{:S(2)}) copy-start(bf16[4096]{0:T(1024)(128)(2,1)} %param.8) | copy-start | bytes 24580
  6.5 50.9 %reduce-scatter.2.cloned.1.call-start = ((), (), s32[]{:S(2)}) async-start(), calls=%async_computation.3 | async-start | bytes 6291456 | tf_op jit(solution)/shard_map/reduce_scatter | solution.py:24
  16.6 24.1 %copy-start = (s32[1024,1]{0,1:T(1,128)S(1)}, s32[1024,1]{0,1:T(1,128)}, u32[]{:S(2)}) copy-start(s32[1024,1]{0,1:T(1,128)} %param.11) | copy-start | bytes 12292
  50.9 25.9 %all-to-all-start = ((s32[16,1,192]{2,1,0:T(1,128)}), s32[16,1,192]{2,1,0:T(1,128)S(1)}, u32[]{:S(2)}, u32[]{:S(2)}) async-start(s32[16,1,192]{2,1,0:T(1,128)} %all_to_all.9), calls=%async_computation | async-start | bytes 32768 | tf_op jit(solution)/shard_map/all_to_all | solution.py:45
  76.8 6.5 %copy-start.1 = (s32[1,3072]{1,0:T(1,128)S(1)}, s32[1,3072]{1,0:T(1,128)}, u32[]{:S(2)}) copy-start(s32[1,3072]{1,0:T(1,128)} %param.13) | copy-start | bytes 36868
  76.8 145.3 %all-to-all-start.1 = ((bf16[16,192,1024]{2,1,0:T(8,128)(2,1)}), bf16[16,192,1024]{2,1,0:T(8,128)(2,1)}, u32[]{:S(2)}, u32[]{:S(2)}) async-start(bf16[16,192,1024]{2,1,0:T(8,128)(2,1)} %bitcast.25), calls=%async_computation.2 | async-start | bytes 12582912 | tf_op jit(solution)/shard_map/all_to_all | solution.py:42
Sparse Core Ops, SparseCore 0:
  40.9 13.4 reduce-scatter.1
where the time goes:
time: 361 us; the launch traced here: 356 us
  other arithmetic  159 us (44%)
  waiting for transfers between devices  138 us (38%)
  matrix products  24.1 us (7%)
  between operations  13.5 us (4%)
  starting transfers between devices  13 us (4%)
  local copies, waits for them, and re-layouts  5.72 us (2%)
    all_to_all x1, waiting for transfers between devices, shards(): lax.all_to_all(outgoing.astype(jnp.bfloat16), 'dp', split_axis=0, concat_...  138 us
    scatter x1, other arithmetic, shards(): jnp.zeros((n_dp * slot_cap, key_width), jnp.bfloat16).at[slot_table[0]]  127 us
    dot_general x1, matrix products, shards(): product = jnp.dot(normed, projection, preferred_element_type=jnp.float32)  24.1 us
    scatter x1, other arithmetic, shards(): jnp.zeros((n_dp * slot_cap, key_width), jnp.float32).at[flat_pos]  11.1 us
    convert_element_type x1, other arithmetic, shards(): outgoing.astype(jnp.bfloat16)  8.28 us
  transfers between devices with their start and end apart: 3, of which 1 were waited for; matrix products, arithmetic and copies ran while one was open for 8% of the time, Pallas kernels for 0%

commit v1 on v0

v1 whole, which is shorter than its diff:
```python
import functools

import jax
import jax.numpy as jnp
from jax import lax
from jax.experimental import pallas as pl
from jax.experimental.pallas import tpu as pltpu
from jax.sharding import PartitionSpec as P

D = 8192
EPSILON = 1e-05
LANES = 128
MIB = 1024 * 1024
F32 = jnp.float32
BF16 = jnp.bfloat16
I32 = jnp.int32


def iota(shape, dim):
    return lax.broadcasted_iota(I32, shape, dim)


def fit(total, wanted):
    best = 16
    for size in range(16, min(total, wanted) + 1, 16):
        if total % size == 0:
            best = size
    return best


def params(mib):
    return pltpu.CompilerParams(vmem_limit_bytes=mib * MIB)


def partial_kernel(which, hidden, gain, projection, out, total, squares):
    step = pl.program_id(0)
    rows, depth = hidden.shape
    tile = fit(rows, 256)

    @pl.when(step == 0)
    def _():
        total[...] = jnp.zeros_like(total)
        squares[...] = jnp.zeros_like(squares)

    @pl.loop(0, rows // tile)
    def _(i):
        at = pl.ds(pl.multiple_of(i * tile, tile), tile)
        block = hidden[at, :]
        total[at, :] += jnp.dot(block * gain[...], projection[...], preferred_element_type=F32)
        wide = block.astype(F32)
        wide = wide * wide
        part = wide[:, :LANES]
        for lane in range(LANES, depth, LANES):
            part = part + wide[:, lane : lane + LANES]
        squares[at, :] += part

    @pl.when(step == pl.num_programs(0) - 1)
    def _():
        width = total.shape[1]

        @pl.loop(0, rows // tile)
        def _(i):
            at = pl.ds(pl.multiple_of(i * tile, tile), tile)
            out[at, :width] = total[at, :].astype(BF16)
            energy = squares[at, :]
            high = energy.astype(BF16)
            wide = high.astype(F32)
            out[at, width : width + LANES] = high
            out[at, width + LANES :] = jnp.where(wide < 3e38, energy - wide, 0.0).astype(BF16)


def partial_keys(which, hidden, gain, projection, rows):
    depth, width = projection.shape
    block = 1024
    return pl.pallas_call(
        partial_kernel,
        grid_spec=pltpu.PrefetchScalarGridSpec(
            num_scalar_prefetch=1,
            grid=(depth // block,),
            in_specs=[
                pl.BlockSpec((rows, block), lambda k, w: (w[0], k)),
                pl.BlockSpec((1, block), lambda k, w: (0, k)),
                pl.BlockSpec((block, width), lambda k, w: (k, 0)),
            ],
            out_specs=pl.BlockSpec((rows, width + 2 * LANES), lambda k, w: (0, 0)),
            scratch_shapes=[pltpu.VMEM((rows, width), F32), pltpu.VMEM((rows, LANES), F32)],
        ),
        out_shape=jax.ShapeDtypeStruct((rows, width + 2 * LANES), BF16),
        compiler_params=params(32),
        cost_estimate=pl.CostEstimate(
            flops=2 * rows * depth * width,
            bytes_accessed=2 * (rows * depth + depth * width + rows * width),
            transcendentals=0,
        ),
        name="partial_keys",
    )(which, hidden, gain, projection)


def route_kernel(n_dp, cap, owners, lists, place, listed):
    rows = owners.shape[1]
    n_own = 128 if n_dp <= 128 else n_dp
    hot = iota((n_own, rows), 0) == owners[...]
    onehot = hot.astype(F32).astype(BF16)
    before = (iota((rows, rows), 0) < iota((rows, rows), 1)).astype(F32).astype(BF16)
    ranks = jnp.dot(onehot, before, preferred_element_type=F32)
    rank = jnp.sum(jnp.where(hot, ranks, 0.0), axis=0, keepdims=True).astype(I32)
    place[...] = jnp.broadcast_to(owners[...] * cap + rank, place.shape)
    at_rank = (iota((listed.shape[1], rows), 0) == rank).astype(F32).astype(BF16)
    high = (lists[...] // 64).astype(F32)
    low = (lists[...] % 64).astype(F32)

    def by_owner(values):
        picked = jnp.where(hot, values, 0.0).astype(BF16)
        return lax.dot_general(picked, at_rank, (((1,), (1,)), ((), ())), preferred_element_type=F32)

    live = by_owner(jnp.ones_like(high))
    ids = by_owner(high) * 64.0 + by_owner(low)
    found = jnp.where(live > 0.5, ids, -1.0).astype(I32)
    listed[...] = found[:n_dp, :]


def route(owners, lists, n_dp, cap):
    rows = owners.shape[1]
    wide = -(-cap // LANES) * LANES
    return pl.pallas_call(
        functools.partial(route_kernel, n_dp, cap),
        out_shape=(
            jax.ShapeDtypeStruct((8, rows), I32),
            jax.ShapeDtypeStruct((n_dp, wide), I32),
        ),
        compiler_params=params(32),
        cost_estimate=pl.CostEstimate(
            flops=2 * rows * rows * 128, bytes_accessed=rows * 64, transcendentals=0
        ),
        name="route",
    )(owners, lists)


def pack_kernel(own, other, place, out, keys):
    width = keys.shape[1]
    rows = keys.shape[0]
    step = pl.program_id(0)

    @pl.when(step == 0)
    def _():
        tile = fit(rows, 128)

        @pl.loop(0, rows // tile)
        def _(i):
            at = pl.ds(pl.multiple_of(i * tile, tile), tile)
            parts = own[at, width:].astype(F32) + other[at, width:].astype(F32)
            energy = jnp.sum(parts, axis=1, keepdims=True)
            scale = lax.rsqrt(energy * (1.0 / D) + EPSILON)
            terms = own[at, :width].astype(F32) + other[at, :width].astype(F32)
            keys[at, :] = jnp.where(scale > 0.0, terms * scale, 0.0).astype(BF16)

    size = out.shape[0]
    onehot = (iota((size, rows), 0) + step * size == place[0:1, :]).astype(F32).astype(BF16)
    out[...] = jnp.dot(onehot, keys[...], preferred_element_type=F32).astype(BF16)


def pack(own, other, place, total):
    rows = own.shape[0]
    width = own.shape[1] - 2 * LANES
    tile = fit(total, 512)
    return pl.pallas_call(
        pack_kernel,
        grid=(total // tile,),
        in_specs=[
            pl.BlockSpec((rows, width + 2 * LANES), lambda i: (0, 0)),
            pl.BlockSpec((rows, width + 2 * LANES), lambda i: (0, 0)),
            pl.BlockSpec((8, rows), lambda i: (0, 0)),
        ],
        out_specs=pl.BlockSpec((tile, width), lambda i: (i, 0)),
        out_shape=jax.ShapeDtypeStruct((total, width), BF16),
        scratch_shapes=[pltpu.VMEM((rows, width), BF16)],
        compiler_params=params(40),
        cost_estimate=pl.CostEstimate(
            flops=2 * total * rows * width,
            bytes_accessed=2 * width * (2 * rows + total),
            transcendentals=rows,
        ),
        name="pack_keys",
    )(own, other, place)


def centre_kernel(slots, lists, centroids, out):
    size = out.shape[0]
    first = pl.program_id(0) * size
    hit = slots[...] == iota((size, slots.shape[1]), 0) + first
    at = jnp.sum(jnp.where(hit, lists[...] + 1, 0), axis=1, keepdims=True) - 1
    onehot = (iota((size, centroids.shape[0]), 1) == at).astype(F32).astype(BF16)
    out[...] = jnp.dot(onehot, centroids[...], preferred_element_type=F32).astype(BF16)


def centres(slots, lists, centroids):
    count = slots.shape[1]
    n_lists, width = centroids.shape
    tile = fit(count, 256)
    return pl.pallas_call(
        centre_kernel,
        grid=(count // tile,),
        in_specs=[
            pl.BlockSpec((1, count), lambda i: (0, 0)),
            pl.BlockSpec((1, count), lambda i: (0, 0)),
            pl.BlockSpec((n_lists, width), lambda i: (0, 0)),
        ],
        out_specs=pl.BlockSpec((tile, width), lambda i: (i, 0)),
        out_shape=jax.ShapeDtypeStruct((count, width), BF16),
        compiler_params=params(48),
        cost_estimate=pl.CostEstimate(
            flops=2 * count * n_lists * width,
            bytes_accessed=2 * width * (count + n_lists),
            transcendentals=0,
        ),
        name="centroid_rows",
    )(slots, lists, centroids)


def place_kernel(slots, arrived, centre, out):
    size = out.shape[0]
    first = pl.program_id(0) * size
    onehot = (slots[...] == iota((size, slots.shape[1]), 0) + first).astype(F32).astype(BF16)
    keys = jnp.dot(onehot, arrived[...], preferred_element_type=F32)
    out[...] = (keys - centre[...].astype(F32)).astype(BF16)


def place_rows(slots, arrived, centre):
    count, width = centre.shape
    n_rows = arrived.shape[0]
    tile = fit(count, 256)
    return pl.pallas_call(
        place_kernel,
        grid=(count // tile,),
        in_specs=[
            pl.BlockSpec((1, n_rows), lambda i: (0, 0)),
            pl.BlockSpec((n_rows, width), lambda i: (0, 0)),
            pl.BlockSpec((tile, width), lambda i: (i, 0)),
        ],
        out_specs=pl.BlockSpec((tile, width), lambda i: (i, 0)),
        out_shape=jax.ShapeDtypeStruct((count, width), BF16),
        compiler_params=params(48),
        cost_estimate=pl.CostEstimate(
            flops=2 * count * n_rows * width,
            bytes_accessed=2 * width * (2 * count + n_rows),
            transcendentals=0,
        ),
        name="residual_rows",
    )(slots, arrived, centre)


def shards(hidden, norm_gain, projection, centroids, owners, local_list, slot_table):
    n_dp = lax.axis_size("dp")
    me = lax.axis_index("tp").astype(I32)
    rows = owners.shape[0]
    width = projection.shape[1]
    cap = slot_table.shape[1] // n_dp
    gain = norm_gain.reshape(1, -1)

    place, listed = route(owners.reshape(1, rows), local_list.reshape(1, rows), n_dp, cap)
    lists = lax.all_to_all(listed, "dp", split_axis=0, concat_axis=0, tiled=True)
    lists = lists[:, :cap].reshape(1, n_dp * cap)

    for_other = partial_keys((1 - me).reshape(1), hidden, gain, projection, rows)
    other = lax.ppermute(for_other, "tp", [(0, 1), (1, 0)])
    own = partial_keys(me.reshape(1), hidden, gain, projection, rows)
    outgoing = pack(own, other, place, n_dp * cap)
    arrived = lax.all_to_all(
        outgoing.reshape(n_dp, cap, width), "dp", split_axis=0, concat_axis=0, tiled=True
    ).reshape(n_dp * cap, width)

    centre = centres(slot_table, lists, centroids)
    live = jnp.where(lists >= 0, slot_table, -1)
    return place_rows(live, arrived, centre)


def solution(mesh):
    placed = (
        P("dp", "tp"),
        P("tp"),
        P("tp", None),
        P("dp", None),
        P(("dp", "tp"), None),
        P(("dp", "tp")),
        P(("dp", "tp"), None),
    )
    return jax.shard_map(
        shards, mesh=mesh, in_specs=placed, out_specs=P(("dp", "tp"), None), check_vma=False
    )
```

time: 361 us -> 233 us (0.65)
  other arithmetic: 159 us -> 0.02 us
  Pallas kernels: 0 us -> 101 us
  waiting for transfers between devices: 138 us -> 104 us
  matrix products: 24.1 us -> 0 us
  between operations: 13.5 us -> 0.08 us
  local copies, waits for them, and re-layouts: 5.72 us -> 10.9 us
    scatter x2 -> x0, other arithmetic: 138 us -> none  [the longest x1 127 us: shards(): jnp.zeros((n_dp * slot_cap, key_width), jnp.bfloat16).at[slot_table[0]]]
    pallas_call x0 -> x6, Pallas kernels: none -> 101 us  [the longest x1 36.4 us: centres(): pl.pallas_call(centre_kernel, grid=(count // tile,), in_specs=[pl.BlockSp...]
    all_to_all x2, waiting for transfers between devices: 138 us -> 104 us  [the longest x1 103 us: shards(): lax.all_to_all(outgoing.reshape(n_dp, cap, width), 'dp', split_axis=0, co...]
    dot_general x1 -> x0, matrix products: 24.1 us -> none  [shards(): product = jnp.dot(normed, projection, preferred_element_type=jnp.float32)]
    unnamed x6 -> x13, local copies, waits for them, and re-layouts: 0.01 us -> 9.46 us
    convert_element_type x3 -> x0, other arithmetic: 8.29 us -> none  [the longest x1 8.28 us: shards(): outgoing.astype(jnp.bfloat16)]
    reduce_sum x2 -> x0, other arithmetic: 7.23 us -> none  [the longest x1 7.21 us: shards(): energy = lax.psum(jnp.sum(values * values, axis=1), 'tp')]
    another operation x2 -> x0, other arithmetic: 4.55 us -> none
  transfers between devices with their start and end apart: 3 -> 3, of which waited for: 1 -> 1; matrix products, arithmetic and copies ran while one was open for 8% -> 0% of each run, Pallas kernels for 0% -> 26%
where the time goes in v1:
time: 233 us; the launch traced here: 229 us
  waiting for transfers between devices  104 us (45%)
  Pallas kernels  101 us (43%)
  starting transfers between devices  13.6 us (6%)
  local copies, waits for them, and re-layouts  10.9 us (5%)
    all_to_all x1, waiting for transfers between devices, shards(): lax.all_to_all(outgoing.reshape(n_dp, cap, width), 'dp', split_axis=0, co...  103 us
    pallas_call x1, Pallas kernels, centres(): pl.pallas_call(centre_kernel, grid=(count // tile,), in_specs=[pl.BlockSp...  36.4 us
    pallas_call x2, Pallas kernels, partial_keys(): pl.pallas_call(partial_kernel, grid_spec=pltpu.PrefetchScalarGridSpec(num...  29.5 us
    pallas_call x1, Pallas kernels, place_rows(): pl.pallas_call(place_kernel, grid=(count // tile,), in_specs=[pl.BlockSpe...  25.5 us
    unnamed x13, local copies, waits for them, and re-layouts  9.46 us
    pallas_call x1, Pallas kernels, pack(): pl.pallas_call(pack_kernel, grid=(total // tile,), in_specs=[pl.BlockSpec...  8.78 us
    all_to_all x1, starting transfers between devices, shards(): lax.all_to_all(listed, 'dp', split_axis=0, concat_axis=0, tiled=True)  6.49 us
    all_to_all x1, starting transfers between devices, shards(): lax.all_to_all(outgoing.reshape(n_dp, cap, width), 'dp', split_axis=0, co...  6.48 us
  transfers between devices with their start and end apart: 3, of which 1 were waited for; matrix products, arithmetic and copies ran while one was open for 0% of the time, Pallas kernels for 26%

profile of v1, /device:TPU:21, one launch (start us, length us, event | category | flops | bytes accessed | tf_op | source)
XLA Modules:
  0.0 229.3 jit_solution(1851916197187312434)
XLA Ops:
  0.0 0.7 reshape.42.gain
  0.7 0.0 copy-start.2
  0.7 3.4 %copy-done.2 = bf16[4096,1024]{1,0:T(8,128)(2,1)S(1)} copy-done((bf16[4096,1024]{1,0:T(8,128)(2,1)S(1)}, bf16[4096,1024]{1,0:T(8,128)(2,1)}, u32[]{:S(2)}) %copy-start.2) | copy-done | bytes 8388632
  4.1 0.0 copy-start.4
  4.1 15.5 %partial_keys.3 = bf16[1024,1280]{1,0:T(8,128)(2,1)} custom-call(s32[1]{0:T(128)} %bitcast.4.which, bf16[2048,4096]{1,0:T(8,128)(2,1)} %hidden.3, bf16[1,4096]{1,0:T(2,128)(2,1)S(1)} %reshape.42.gain, bf16[4096,1024]{1,0:T(8,128)(2,1)S(1)} %copy-done.2), custom_call_target="tpu_custom_call" | custom-call | flops 8589934592 | bytes 18874368 | tf_op jit(solution)/shard_map/partial_keys/pallas_call | solution.py:75
  19.6 0.7 collective-permute-start
  20.3 0.0 copy-done.4
  20.3 0.0 copy-done.5
  20.3 1.1 route.1
  21.3 0.6 copy.8
  22.0 6.5 %all-to-all-start = ((s32[16,1,256]{2,1,0:T(1,128)}), s32[16,1,256]{2,1,0:T(1,128)S(1)}, u32[]{:S(2)}, u32[]{:S(2)}) async-start(s32[16,1,256]{2,1,0:T(1,128)} %copy.8), calls=%async_computation | async-start | bytes 32768 | tf_op jit(solution)/shard_map/all_to_all | solution.py:261
  28.5 3.4 %copy-done.3 = bf16[4096,1024]{1,0:T(8,128)(2,1)S(1)} copy-done((bf16[4096,1024]{1,0:T(8,128)(2,1)S(1)}, bf16[4096,1024]{1,0:T(8,128)(2,1)}, u32[]{:S(2)}) %copy-start.3) | copy-done | bytes 8388632
  31.8 14.0 %partial_keys.2.own = bf16[1024,1280]{1,0:T(8,128)(2,1)S(1)} custom-call(s32[1]{0:T(128)} %bitcast.3.which, bf16[2048,4096]{1,0:T(8,128)(2,1)} %hidden.3, bf16[1,4096]{1,0:T(2,128)(2,1)S(1)} %reshape.42.gain, bf16[4096,1024]{1,0:T(8,128)(2,1)S(1)} %copy-done.3), custom_call_target="tpu_custom_call" | custom-call | flops 8589934592 | bytes 18874368 | tf_op jit(solution)/shard_map/partial_keys/pallas_call | solution.py:75
  45.8 0.0 collective-permute-done.other
  45.8 8.8 %pack_keys.1 = bf16[3072,1024]{1,0:T(8,128)(2,1)S(1)} custom-call(bf16[1024,1280]{1,0:T(8,128)(2,1)S(1)} %partial_keys.2.own, bf16[1024,1280]{1,0:T(8,128)(2,1)S(1)} %collective-permute-done.other, s32[8,1024]{1,0:T(8,128)S(1)} %get-tuple-element.8.place), custom_call_target="tpu_custom_call" | custom-call | flops 6442450944 | bytes 10485760 | tf_op jit(solution)/shard_map/pack_keys/pallas_call | solution.py:166
  54.6 0.0 copy-start
  54.6 2.7 %copy-done = bf16[3072,1024]{1,0:T(8,128)(2,1)} copy-done((bf16[3072,1024]{1,0:T(8,128)(2,1)}, bf16[3072,1024]{1,0:T(8,128)(2,1)S(1)}, u32[]{:S(2)}) %copy-start) | copy-done | bytes 6291480
  57.3 0.0 all-to-all-done
  57.3 6.5 %all-to-all-start.1 = ((bf16[16,192,1024]{2,1,0:T(8,128)(2,1)}), bf16[16,192,1024]{2,1,0:T(8,128)(2,1)}, u32[]{:S(2)}, u32[]{:S(2)}) async-start(bf16[16,192,1024]{2,1,0:T(8,128)(2,1)} %bitcast.11), calls=%async_computation.1 | async-start | bytes 12582912 | tf_op jit(solution)/shard_map/all_to_all | solution.py:268
  63.8 0.1 reshape.40.lists
  63.9 0.0 copy-done.1
  63.9 36.4 %centroid_rows.1.centre = bf16[3072,1024]{1,0:T(8,128)(2,1)} custom-call(s32[1,3072]{1,0:T(1,128)S(1)} %copy-done.1, s32[1,3072]{1,0:T(1,128)S(1)} %reshape.40.lists, bf16[4096,1024]{1,0:T(8,128)(2,1)} %centroids.1), custom_call_target="tpu_custom_call" | custom-call | flops 25769803776 | bytes 14680064 | tf_op jit(solution)/shard_map/centroid_rows/pallas_call | solution.py:200
  100.3 103.5 %all-to-all-done.1 = bf16[16,192,1024]{2,1,0:T(8,128)(2,1)} async-done(((bf16[16,192,1024]{2,1,0:T(8,128)(2,1)}), bf16[16,192,1024]{2,1,0:T(8,128)(2,1)}, u32[]{:S(2)}, u32[]{:S(2)}) %all-to-all-start.1) | async-done | bytes 6291488 | tf_op jit(solution)/shard_map/all_to_all | solution.py:268
  203.8 25.5 %residual_rows.1 = bf16[3072,1024]{1,0:T(8,128)(2,1)} custom-call(s32[1,3072]{1,0:T(1,128)S(1)} %compare_select_fusion.slots, bf16[3072,1024]{1,0:T(8,128)(2,1)} %bitcast.6.arrived, bf16[3072,1024]{1,0:T(8,128)(2,1)} %centroid_rows.1.centre), custom_call_target="tpu_custom_call" | custom-call | flops 19327352832 | bytes 18874368 | tf_op jit(solution)/shard_map/residual_rows/pallas_call | solution.py:232
  (5 shorter events, 0.0 us)
Async XLA Ops:
  0.7 3.4 %copy-start.2 = (bf16[4096,1024]{1,0:T(8,128)(2,1)S(1)}, bf16[4096,1024]{1,0:T(8,128)(2,1)}, u32[]{:S(2)}) copy-start(bf16[4096,1024]{1,0:T(8,128)(2,1)} %projection.3) | copy-start | bytes 25165828
  4.1 16.2 %copy-start.4 = (s32[1024,1]{0,1:T(1,128)S(1)}, s32[1024,1]{0,1:T(1,128)}, u32[]{:S(2)}) copy-start(s32[1024,1]{0,1:T(1,128)} %param.11) | copy-start | bytes 12292
  4.1 16.2 %copy-start.5 = (s32[1024]{0:T(1024)S(1)}, s32[1024]{0:T(1024)}, u32[]{:S(2)}) copy-start(s32[1024]{0:T(1024)} %param.12) | copy-start | bytes 12292
  19.6 26.2 %collective-permute-start = (bf16[1024,1280]{1,0:T(8,128)(2,1)}, bf16[1024,1280]{1,0:T(8,128)(2,1)S(1)}, u32[]{:S(2)}, u32[]{:S(2)}) collective-permute-start(bf16[1024,1280]{1,0:T(8,128)(2,1)} %partial_keys.3), channel_id=1, source_target_pairs={{0,16},{16,0},{1,17},{17,1},{2,18},{18,2},{3,19},{19,3},{4,20},{20... | collective-permute-start | bytes 7864328 | tf_op jit(solution)/shard_map/ppermute | solution.py:265
  22.0 35.4 %all-to-all-start = ((s32[16,1,256]{2,1,0:T(1,128)}), s32[16,1,256]{2,1,0:T(1,128)S(1)}, u32[]{:S(2)}, u32[]{:S(2)}) async-start(s32[16,1,256]{2,1,0:T(1,128)} %copy.8), calls=%async_computation | async-start | bytes 32768 | tf_op jit(solution)/shard_map/all_to_all | solution.py:261
  28.5 3.4 %copy-start.3 = (bf16[4096,1024]{1,0:T(8,128)(2,1)S(1)}, bf16[4096,1024]{1,0:T(8,128)(2,1)}, u32[]{:S(2)}) copy-start(bf16[4096,1024]{1,0:T(8,128)(2,1)} %projection.3) | copy-start | bytes 25165828
  54.6 2.7 %copy-start = (bf16[3072,1024]{1,0:T(8,128)(2,1)}, bf16[3072,1024]{1,0:T(8,128)(2,1)S(1)}, u32[]{:S(2)}) copy-start(bf16[3072,1024]{1,0:T(8,128)(2,1)S(1)} %pack_keys.1) | copy-start | bytes 18874372
  57.3 6.6 %copy-start.1 = (s32[1,3072]{1,0:T(1,128)S(1)}, s32[1,3072]{1,0:T(1,128)}, u32[]{:S(2)}) copy-start(s32[1,3072]{1,0:T(1,128)} %slots.1) | copy-start | bytes 36868
  57.3 146.5 %all-to-all-start.1 = ((bf16[16,192,1024]{2,1,0:T(8,128)(2,1)}), bf16[16,192,1024]{2,1,0:T(8,128)(2,1)}, u32[]{:S(2)}, u32[]{:S(2)}) async-start(bf16[16,192,1024]{2,1,0:T(8,128)(2,1)} %bitcast.11), calls=%async_computation.1 | async-start | bytes 12582912 | tf_op jit(solution)/shard_map/all_to_all | solution.py:268

commit v2 on v1

v2 whole, which is shorter than its diff:
```python
import functools

import jax
import jax.numpy as jnp
from jax import lax
from jax.experimental import pallas as pl
from jax.experimental.pallas import tpu as pltpu
from jax.sharding import PartitionSpec as P

D = 8192
EPSILON = 1e-05
LANES = 128
MIB = 1024 * 1024
PARTS = 2
F32 = jnp.float32
BF16 = jnp.bfloat16
I32 = jnp.int32


def iota(shape, dim):
    return lax.broadcasted_iota(I32, shape, dim)


def fit(total, wanted):
    best = 16
    for size in range(16, min(total, wanted) + 1, 16):
        if total % size == 0:
            best = size
    return best


def params(mib):
    return pltpu.CompilerParams(vmem_limit_bytes=mib * MIB)


def partial_kernel(which, hidden, gain, projection, out, total, squares):
    step = pl.program_id(0)
    rows, depth = hidden.shape
    tile = fit(rows, 1024)

    @pl.when(step == 0)
    def _():
        total[...] = jnp.zeros_like(total)
        squares[...] = jnp.zeros_like(squares)

    @pl.loop(0, rows // tile)
    def _(i):
        at = pl.ds(pl.multiple_of(i * tile, tile), tile)
        block = hidden[at, :]
        total[at, :] += jnp.dot(block * gain[...], projection[...], preferred_element_type=F32)
        wide = block.astype(F32)
        wide = wide * wide
        part = wide[:, :LANES]
        for lane in range(LANES, depth, LANES):
            part = part + wide[:, lane : lane + LANES]
        squares[at, :] += part

    @pl.when(step == pl.num_programs(0) - 1)
    def _():
        width = total.shape[1]

        @pl.loop(0, rows // tile)
        def _(i):
            at = pl.ds(pl.multiple_of(i * tile, tile), tile)
            out[at, :width] = total[at, :].astype(BF16)
            if out.shape[1] > width:
                energy = squares[at, :]
                high = energy.astype(BF16)
                wide = high.astype(F32)
                out[at, width : width + LANES] = high
                out[at, width + LANES :] = jnp.where(wide < 3e38, energy - wide, 0.0).astype(BF16)


def partial_keys(which, hidden, gain, projection, rows, part, parts):
    depth, width = projection.shape
    width = width // parts
    block = 1024
    wide = width + (2 * LANES if part == 0 else 0)
    return pl.pallas_call(
        partial_kernel,
        grid_spec=pltpu.PrefetchScalarGridSpec(
            num_scalar_prefetch=1,
            grid=(depth // block,),
            in_specs=[
                pl.BlockSpec((rows, block), lambda k, w: (w[0], k)),
                pl.BlockSpec((1, block), lambda k, w: (0, k)),
                pl.BlockSpec((block, width), lambda k, w: (k, part)),
            ],
            out_specs=pl.BlockSpec((rows, wide), lambda k, w: (0, 0)),
            scratch_shapes=[pltpu.VMEM((rows, width), F32), pltpu.VMEM((rows, LANES), F32)],
        ),
        out_shape=jax.ShapeDtypeStruct((rows, wide), BF16),
        compiler_params=params(60),
        cost_estimate=pl.CostEstimate(
            flops=2 * rows * depth * width,
            bytes_accessed=2 * (rows * depth + depth * width + rows * width),
            transcendentals=0,
        ),
        name="partial_keys",
    )(which, hidden, gain, projection)


def route_kernel(n_dp, cap, owners, lists, place, listed):
    rows = owners.shape[1]
    n_own = 128 if n_dp <= 128 else n_dp
    hot = iota((n_own, rows), 0) == owners[...]
    onehot = hot.astype(F32).astype(BF16)
    before = (iota((rows, rows), 0) < iota((rows, rows), 1)).astype(F32).astype(BF16)
    ranks = jnp.dot(onehot, before, preferred_element_type=F32)
    rank = jnp.sum(jnp.where(hot, ranks, 0.0), axis=0, keepdims=True).astype(I32)
    place[...] = jnp.broadcast_to(owners[...] * cap + rank, place.shape)
    at_rank = (iota((listed.shape[1], rows), 0) == rank).astype(F32).astype(BF16)
    high = (lists[...] // 64).astype(F32)
    low = (lists[...] % 64).astype(F32)

    def by_owner(values):
        picked = jnp.where(hot, values, 0.0).astype(BF16)
        return lax.dot_general(picked, at_rank, (((1,), (1,)), ((), ())), preferred_element_type=F32)

    live = by_owner(jnp.ones_like(high))
    ids = by_owner(high) * 64.0 + by_owner(low)
    found = jnp.where(live > 0.5, ids, -1.0).astype(I32)
    listed[...] = found[:n_dp, :]


def route(owners, lists, n_dp, cap):
    rows = owners.shape[1]
    wide = -(-cap // LANES) * LANES
    return pl.pallas_call(
        functools.partial(route_kernel, n_dp, cap),
        out_shape=(
            jax.ShapeDtypeStruct((8, rows), I32),
            jax.ShapeDtypeStruct((n_dp, wide), I32),
        ),
        compiler_params=params(32),
        cost_estimate=pl.CostEstimate(
            flops=2 * rows * rows * 128, bytes_accessed=rows * 64, transcendentals=0
        ),
        name="route",
    )(owners, lists)


def pack_kernel(own, other, own_first, other_first, place, out, keys):
    rows, width = keys.shape
    step = pl.program_id(0)

    @pl.when(step == 0)
    def _():
        tile = fit(rows, 128)

        @pl.loop(0, rows // tile)
        def _(i):
            at = pl.ds(pl.multiple_of(i * tile, tile), tile)
            parts = own_first[at, width:].astype(F32) + other_first[at, width:].astype(F32)
            energy = jnp.sum(parts, axis=1, keepdims=True)
            scale = lax.rsqrt(energy * (1.0 / D) + EPSILON)
            terms = own[at, :width].astype(F32) + other[at, :width].astype(F32)
            keys[at, :] = jnp.where(scale > 0.0, terms * scale, 0.0).astype(BF16)

    size = out.shape[0]
    onehot = (iota((size, rows), 0) + step * size == place[0:1, :]).astype(F32).astype(BF16)
    out[...] = jnp.dot(onehot, keys[...], preferred_element_type=F32).astype(BF16)


def pack(place, sums, first, total):
    rows = place.shape[1]
    width = first[0].shape[1] - 2 * LANES
    tile = fit(total, 768)
    whole = lambda i: (0, 0)
    operands = [*sums, *first, place]
    return pl.pallas_call(
        pack_kernel,
        grid=(total // tile,),
        in_specs=[pl.BlockSpec(part.shape, whole) for part in operands],
        out_specs=pl.BlockSpec((tile, width), lambda i: (i, 0)),
        out_shape=jax.ShapeDtypeStruct((total, width), BF16),
        scratch_shapes=[pltpu.VMEM((rows, width), BF16)],
        compiler_params=params(60),
        cost_estimate=pl.CostEstimate(
            flops=2 * total * rows * width,
            bytes_accessed=2 * width * (4 * rows + total),
            transcendentals=rows,
        ),
        name="pack_keys",
    )(*operands)


def centre_kernel(n_in, slots, lists, centroids, out, table, placed):
    step = pl.program_id(0)
    block = centroids.shape[0]
    n_lists = n_in * block
    chunks = centroids.shape[1] // LANES
    count = placed.shape[0] // chunks
    size = out.shape[0]

    @pl.when(step == 0)
    def _():
        table[pl.ds(n_lists * chunks, chunks), :] = jnp.zeros((chunks, LANES), F32)

    @pl.when(step < n_in)
    def _():
        @pl.loop(0, block // 16)
        def _(i):
            wide = centroids[pl.ds(pl.multiple_of(i * 16, 16), 16), :].astype(F32)
            for top in range(0, 16, 8):
                first = (step * block + i * 16 + top) * chunks
                for c in range(chunks):
                    part = wide[top : top + 8, c * LANES : (c + 1) * LANES]
                    table[pl.ds(first + c, 8, stride=chunks), :] = part

    @pl.when(step == n_in)
    def _():
        @pl.loop(0, count // 16)
        def _(i):
            found = []
            for u in range(16):
                a = i * 16 + u
                row = table[pl.ds(pl.multiple_of(lists[a], chunks), chunks), :]
                found.append((slots[a], row))
            for at, row in found:
                placed[pl.ds(pl.multiple_of(at, chunks), chunks), :] = -row

    @pl.when(step >= n_in)
    def _():
        @pl.loop(0, size // 16)
        def _(i):
            rows = []
            for top in range(0, 16, 8):
                first = ((step - n_in) * size + i * 16 + top) * chunks
                rows.append(
                    jnp.concatenate(
                        [placed[pl.ds(first + c, 8, stride=chunks), :] for c in range(chunks)], axis=1
                    )
                )
            out[pl.ds(pl.multiple_of(i * 16, 16), 16), :] = jnp.concatenate(rows, axis=0).astype(BF16)


def centres(slots, lists, centroids):
    count = slots.shape[0]
    n_lists, width = centroids.shape
    slots = slots * (width // LANES)
    lists = jnp.where(lists < 0, n_lists, lists) * (width // LANES)
    block, size = fit(n_lists, 512), fit(count, 512)
    n_in = n_lists // block
    chunks = width // LANES
    return pl.pallas_call(
        functools.partial(centre_kernel, n_in),
        grid_spec=pltpu.PrefetchScalarGridSpec(
            num_scalar_prefetch=2,
            grid=(n_in + count // size,),
            in_specs=[pl.BlockSpec((block, width), lambda i, s, l: (jnp.minimum(i, n_in - 1), 0))],
            out_specs=pl.BlockSpec((size, width), lambda i, s, l: (jnp.maximum(i - n_in, 0), 0)),
            scratch_shapes=[
                pltpu.VMEM(((n_lists + 1) * chunks, LANES), F32),
                pltpu.VMEM((count * chunks, LANES), F32),
            ],
        ),
        out_shape=jax.ShapeDtypeStruct((count, width), BF16),
        compiler_params=params(60),
        cost_estimate=pl.CostEstimate(
            flops=6400 * count * width, bytes_accessed=4 * count * width, transcendentals=0
        ),
        name="centroid_rows",
    )(slots, lists, centroids)


def place_kernel(slots, before, arrived, out):
    tile = out.shape[0]
    first = pl.program_id(0) * tile
    onehot = (slots[...] == iota((tile, slots.shape[1]), 0) + first).astype(F32).astype(BF16)
    keys = jnp.dot(onehot, arrived[...], preferred_element_type=F32)
    out[...] = (keys + before[...].astype(F32)).astype(BF16)


def place_rows(slots, arrived, before, part):
    count = before.shape[0]
    n_rows, width = arrived.shape
    tile = fit(count, 512)
    return pl.pallas_call(
        place_kernel,
        grid=(count // tile,),
        in_specs=[
            pl.BlockSpec((1, n_rows), lambda i: (0, 0)),
            pl.BlockSpec((tile, width), lambda i: (i, part)),
            pl.BlockSpec((n_rows, width), lambda i: (0, 0)),
        ],
        out_specs=pl.BlockSpec((tile, width), lambda i: (i, part)),
        out_shape=jax.ShapeDtypeStruct(before.shape, BF16),
        input_output_aliases={1: 0},
        compiler_params=params(60),
        cost_estimate=pl.CostEstimate(
            flops=2 * count * n_rows * width,
            bytes_accessed=2 * width * (2 * count + n_rows),
            transcendentals=0,
        ),
        name="residual_rows",
    )(slots, before, arrived)


def shards(hidden, norm_gain, projection, centroids, owners, local_list, slot_table):
    n_dp = lax.axis_size("dp")
    me = lax.axis_index("tp").astype(I32)
    rows = owners.shape[0]
    cap = slot_table.shape[1] // n_dp
    gain = norm_gain.reshape(1, -1)

    def exchange(block):
        block = block.reshape(n_dp, cap, -1)
        got = lax.all_to_all(block, "dp", split_axis=0, concat_axis=0, tiled=True)
        return got.reshape(n_dp * cap, -1)

    place, listed = route(owners.reshape(1, rows), local_list.reshape(1, rows), n_dp, cap)
    lists = lax.all_to_all(listed, "dp", split_axis=0, concat_axis=0, tiled=True)

    sums, arrived = [], []
    for part in range(PARTS):
        for_other = partial_keys((1 - me).reshape(1), hidden, gain, projection, rows, part, PARTS)
        other = lax.ppermute(for_other, "tp", [(0, 1), (1, 0)])
        own = partial_keys(me.reshape(1), hidden, gain, projection, rows, part, PARTS)
        sums.append((own, other))
        out = pack(place, sums[part], sums[0], n_dp * cap)
        if part == 0:
            out, lists = lax.optimization_barrier((out, lists))
        arrived.append(exchange(out))

    lists = lists[:, :cap].reshape(-1)
    total = centres(slot_table.reshape(-1), lists, centroids)
    slots = jnp.where(lists >= 0, slot_table.reshape(-1), -1).reshape(1, -1)
    for part in range(PARTS):
        total = place_rows(slots, arrived[part], total, part)
    return total


def solution(mesh):
    placed = (
        P("dp", "tp"),
        P("tp"),
        P("tp", None),
        P("dp", None),
        P(("dp", "tp"), None),
        P(("dp", "tp")),
        P(("dp", "tp"), None),
    )
    return jax.shard_map(
        shards, mesh=mesh, in_specs=placed, out_specs=P(("dp", "tp"), None), check_vma=False
    )
```

time: 233 us -> 208 us (0.89)
  waiting for transfers between devices: 104 us -> 76.1 us
  starting transfers between devices: 13.6 us -> 21 us
  local copies, waits for them, and re-layouts: 10.9 us -> 5.58 us
    all_to_all x1 -> x2, waiting for transfers between devices: 103 us -> 76.1 us  [exchange(): got = lax.all_to_all(block, 'dp', split_axis=0, concat_axis=0, tiled=True)]
    pallas_call x1, Pallas kernels: 36.4 us -> 18.6 us  [centres(): pl.pallas_call(functools.partial(centre_kernel, n_in), grid_spec=pltpu.Pr...]
    pallas_call x1 -> x2, Pallas kernels: 8.78 us -> 17.3 us  [pack(): pl.pallas_call(pack_kernel, grid=(total // tile,), in_specs=[pl.BlockSpec...]
    pallas_call x2 -> x4, Pallas kernels: 29.5 us -> 36.3 us  [partial_keys(): pl.pallas_call(partial_kernel, grid_spec=pltpu.PrefetchScalarGridSpec(num...]
    all_to_all x1 -> x2, starting transfers between devices: 6.48 us -> 12.7 us  [exchange(): got = lax.all_to_all(block, 'dp', split_axis=0, concat_axis=0, tiled=True)]
    unnamed x13, local copies, waits for them, and re-layouts: 9.46 us -> 3.5 us
    pallas_call x1 -> x2, Pallas kernels: 25.5 us -> 27.4 us  [place_rows(): pl.pallas_call(place_kernel, grid=(count // tile,), in_specs=[pl.BlockSpe...]
  transfers between devices with their start and end apart: 3 -> 5, of which waited for: 1 -> 2; matrix products, arithmetic and copies ran while one was open for 0% -> 1% of each run, Pallas kernels for 26% -> 34%
where the time goes in v2:
time: 208 us; the launch traced here: 205 us
  Pallas kernels  101 us (49%)
  waiting for transfers between devices  76.1 us (37%)
  starting transfers between devices  21 us (10%)
  local copies, waits for them, and re-layouts  5.58 us (3%)
    all_to_all x2, waiting for transfers between devices, exchange(): got = lax.all_to_all(block, 'dp', split_axis=0, concat_axis=0, tiled=True)  76.1 us
    pallas_call x4, Pallas kernels, partial_keys(): pl.pallas_call(partial_kernel, grid_spec=pltpu.PrefetchScalarGridSpec(num...  36.3 us
    pallas_call x2, Pallas kernels, place_rows(): pl.pallas_call(place_kernel, grid=(count // tile,), in_specs=[pl.BlockSpe...  27.4 us
    pallas_call x1, Pallas kernels, centres(): pl.pallas_call(functools.partial(centre_kernel, n_in), grid_spec=pltpu.Pr...  18.6 us
    pallas_call x2, Pallas kernels, pack(): pl.pallas_call(pack_kernel, grid=(total // tile,), in_specs=[pl.BlockSpec...  17.3 us
    all_to_all x2, starting transfers between devices, exchange(): got = lax.all_to_all(block, 'dp', split_axis=0, concat_axis=0, tiled=True)  12.7 us
    all_to_all x1, starting transfers between devices, shards(): lax.all_to_all(listed, 'dp', split_axis=0, concat_axis=0, tiled=True)  6.5 us
  transfers between devices with their start and end apart: 5, of which 2 were waited for; matrix products, arithmetic and copies ran while one was open for 1% of the time, Pallas kernels for 34%

profile of v2, /device:TPU:21, one launch (start us, length us, event | category | flops | bytes accessed | tf_op | source)
XLA Modules:
  0.0 204.7 jit_solution(3917584357380670500)
XLA Ops:
  0.0 1.3 reshape.52.gain
  1.3 9.2 %partial_keys.5 = bf16[1024,768]{1,0:T(8,128)(2,1)} custom-call(s32[1]{0:T(128)} %bitcast.1.which, bf16[2048,4096]{1,0:T(8,128)(2,1)} %hidden.7, bf16[1,4096]{1,0:T(2,128)(2,1)} %reshape.52.gain, bf16[4096,1024]{1,0:T(8,128)(2,1)} %projection.7), custom_call_target="tpu_custom_call" | custom-call | flops 4294967296 | bytes 13631488 | tf_op jit(solution)/shard_map/partial_keys/pallas_call | solution.py:79
  10.5 0.7 collective-permute-start
  11.2 1.1 route.1
  12.3 0.6 copy-done.2
  12.9 0.6 copy.10
  13.5 6.5 %all-to-all-start = ((s32[16,1,256]{2,1,0:T(1,128)}), s32[16,1,256]{2,1,0:T(1,128)S(1)}, u32[]{:S(2)}, u32[]{:S(2)}) async-start(s32[16,1,256]{2,1,0:T(1,128)} %copy.10), calls=%async_computation | async-start | bytes 32768 | tf_op jit(solution)/shard_map/all_to_all | solution.py:313
  20.0 9.2 %partial_keys.4.own.own_first = bf16[1024,768]{1,0:T(8,128)(2,1)} custom-call(s32[1]{0:T(128)} %bitcast.which, bf16[2048,4096]{1,0:T(8,128)(2,1)} %hidden.7, bf16[1,4096]{1,0:T(2,128)(2,1)} %reshape.52.gain, bf16[4096,1024]{1,0:T(8,128)(2,1)} %projection.7), custom_call_target="tpu_custom_call" | custom-call | flops 4294967296 | bytes 13631488 | tf_op jit(solution)/shard_map/partial_keys/pallas_call | solution.py:79
  29.3 1.2 copy-done.5
  30.4 8.9 %pack_keys.2 = bf16[3072,512]{1,0:T(8,128)(2,1)} custom-call(bf16[1024,768]{1,0:T(8,128)(2,1)} %partial_keys.4.own.own_first, bf16[1024,768]{1,0:T(8,128)(2,1)} %copy-done.5, bf16[1024,768]{1,0:T(8,128)(2,1)} %partial_keys.4.own.own_first, bf16[1024,768]{1,0:T(8,128)(2,1)} %copy-done.5, s32[8,1024]{1,0:T(8,128)} %copy-done.2), custom_call_target="tpu_custom_call" | custom-call | flops 3221225472 | bytes 7340032 | tf_op jit(solution)/shard_map/pack_keys/pallas_call | solution.py:171
  39.3 6.4 %all-to-all-start.1 = ((bf16[16,192,512]{2,1,0:T(8,128)(2,1)}), bf16[16,192,512]{2,1,0:T(8,128)(2,1)S(1)}, u32[]{:S(2)}, u32[]{:S(2)}) async-start(bf16[16,192,512]{2,1,0:T(8,128)(2,1)} %bitcast.19), calls=%async_computation.1 | async-start | bytes 6291456 | tf_op jit(solution)/shard_map/all_to_all | solution.py:309
  45.7 8.9 %partial_keys.7 = bf16[1024,512]{1,0:T(8,128)(2,1)} custom-call(s32[1]{0:T(128)} %bitcast.1.which, bf16[2048,4096]{1,0:T(8,128)(2,1)} %hidden.7, bf16[1,4096]{1,0:T(2,128)(2,1)} %reshape.52.gain, bf16[4096,1024]{1,0:T(8,128)(2,1)} %projection.7), custom_call_target="tpu_custom_call" | custom-call | flops 4294967296 | bytes 13631488 | tf_op jit(solution)/shard_map/partial_keys/pallas_call | solution.py:79
  54.6 1.1 collective-permute-start.1
  55.8 8.9 %partial_keys.6.own = bf16[1024,512]{1,0:T(8,128)(2,1)} custom-call(s32[1]{0:T(128)} %bitcast.which, bf16[2048,4096]{1,0:T(8,128)(2,1)} %hidden.7, bf16[1,4096]{1,0:T(2,128)(2,1)} %reshape.52.gain, bf16[4096,1024]{1,0:T(8,128)(2,1)} %projection.7), custom_call_target="tpu_custom_call" | custom-call | flops 4294967296 | bytes 13631488 | tf_op jit(solution)/shard_map/partial_keys/pallas_call | solution.py:79
  64.7 8.4 %pack_keys.3 = bf16[3072,512]{1,0:T(8,128)(2,1)} custom-call(bf16[1024,512]{1,0:T(8,128)(2,1)} %partial_keys.6.own, bf16[1024,512]{1,0:T(8,128)(2,1)} %collective-permute-done.1.other, bf16[1024,768]{1,0:T(8,128)(2,1)} %partial_keys.4.own.own_first, bf16[1024,768]{1,0:T(8,128)(2,1)} %copy-done.5, s32[8,1024]{1,0:T(8,128)} %copy-done.2), custom_call_target="tpu_custom_call" | custom-call | flops 3221225472 | bytes 7340032 | tf_op jit(solution)/shard_map/pack_keys/pallas_call | solution.py:171
  73.1 41.5 %all-to-all-done.1 = bf16[16,192,512]{2,1,0:T(8,128)(2,1)S(1)} async-done(((bf16[16,192,512]{2,1,0:T(8,128)(2,1)}), bf16[16,192,512]{2,1,0:T(8,128)(2,1)S(1)}, u32[]{:S(2)}, u32[]{:S(2)}) %all-to-all-start.1) | async-done | bytes 3145760 | tf_op jit(solution)/shard_map/all_to_all | solution.py:309
  114.6 1.7 copy-done.3
  116.3 6.4 %all-to-all-start.2 = ((bf16[16,192,512]{2,1,0:T(8,128)(2,1)}), bf16[16,192,512]{2,1,0:T(8,128)(2,1)}, u32[]{:S(2)}, u32[]{:S(2)}) async-start(bf16[16,192,512]{2,1,0:T(8,128)(2,1)} %bitcast.18), calls=%async_computation.2 | async-start | bytes 6291456 | tf_op jit(solution)/shard_map/all_to_all | solution.py:309
  122.9 0.6 fusion.lists
  123.5 0.6 broadcast_multiply_fusion
  124.1 18.6 %centroid_rows.1.before = bf16[3072,1024]{1,0:T(8,128)(2,1)} custom-call(s32[3072]{0:T(1024)} %bitcast.22, s32[3072]{0:T(1024)} %fusion.lists, bf16[4096,1024]{1,0:T(8,128)(2,1)} %centroids.1), custom_call_target="tpu_custom_call" | custom-call | flops 20132659200 | bytes 12582912 | tf_op jit(solution)/shard_map/centroid_rows/pallas_call | solution.py:246
  142.7 13.7 %residual_rows.2.before = bf16[3072,1024]{1,0:T(8,128)(2,1)} custom-call(s32[1,3072]{1,0:T(1,128)} %get-tuple-element.14.slots, bf16[3072,1024]{1,0:T(8,128)(2,1)} %centroid_rows.1.before, bf16[3072,512]{1,0:T(8,128)(2,1)} %bitcast.17), custom_call_target="tpu_custom_call", output_to_operand_aliasing={{}: (1, {})} | custom-call | flops 9663676416 | bytes 9437184 | tf_op jit(solution)/shard_map/residual_rows/pallas_call | solution.py:279
  156.4 34.6 %all-to-all-done.2 = bf16[16,192,512]{2,1,0:T(8,128)(2,1)} async-done(((bf16[16,192,512]{2,1,0:T(8,128)(2,1)}), bf16[16,192,512]{2,1,0:T(8,128)(2,1)}, u32[]{:S(2)}, u32[]{:S(2)}) %all-to-all-start.2) | async-done | bytes 3145760 | tf_op jit(solution)/shard_map/all_to_all | solution.py:309
  191.0 13.7 %residual_rows.3 = bf16[3072,1024]{1,0:T(8,128)(2,1)} custom-call(s32[1,3072]{1,0:T(1,128)} %get-tuple-element.14.slots, bf16[3072,1024]{1,0:T(8,128)(2,1)} %residual_rows.2.before, bf16[3072,512]{1,0:T(8,128)(2,1)} %bitcast.9.arrived), custom_call_target="tpu_custom_call", output_to_operand_aliasing={{}: (1, {})} | custom-call | flops 9663676416 | bytes 9437184 | tf_op jit(solution)/shard_map/residual_rows/pallas_call | solution.py:279
  (16 shorter events, 0.2 us)
Async XLA Ops:
  1.3 9.9 %copy-start = (s32[1024,1]{0,1:T(1,128)S(1)}, s32[1024,1]{0,1:T(1,128)}, u32[]{:S(2)}) copy-start(s32[1024,1]{0,1:T(1,128)} %param.11) | copy-start | bytes 12292
  1.3 9.9 %copy-start.1 = (s32[1024]{0:T(1024)S(1)}, s32[1024]{0:T(1024)}, u32[]{:S(2)}) copy-start(s32[1024]{0:T(1024)} %param.12) | copy-start | bytes 12292
  10.5 18.7 %collective-permute-start = (bf16[1024,768]{1,0:T(8,128)(2,1)}, bf16[1024,768]{1,0:T(8,128)(2,1)S(1)}, u32[]{:S(2)}, u32[]{:S(2)}) collective-permute-start(bf16[1024,768]{1,0:T(8,128)(2,1)} %partial_keys.5), channel_id=1, source_target_pairs={{0,16},{16,0},{1,17},{17,1},{2,18},{18,2},{3,19},{19,3},{4,20},{20... | collective-permute-start | bytes 4718600 | tf_op jit(solution)/shard_map/ppermute | solution.py:318
  12.3 0.6 copy-start.2
  13.5 15.7 %all-to-all-start = ((s32[16,1,256]{2,1,0:T(1,128)}), s32[16,1,256]{2,1,0:T(1,128)S(1)}, u32[]{:S(2)}, u32[]{:S(2)}) async-start(s32[16,1,256]{2,1,0:T(1,128)} %copy.10), calls=%async_computation | async-start | bytes 32768 | tf_op jit(solution)/shard_map/all_to_all | solution.py:313
  29.3 1.2 copy-start.5
  39.3 75.3 %all-to-all-start.1 = ((bf16[16,192,512]{2,1,0:T(8,128)(2,1)}), bf16[16,192,512]{2,1,0:T(8,128)(2,1)S(1)}, u32[]{:S(2)}, u32[]{:S(2)}) async-start(bf16[16,192,512]{2,1,0:T(8,128)(2,1)} %bitcast.19), calls=%async_computation.1 | async-start | bytes 6291456 | tf_op jit(solution)/shard_map/all_to_all | solution.py:309
  54.6 10.1 %collective-permute-start.1 = (bf16[1024,512]{1,0:T(8,128)(2,1)}, bf16[1024,512]{1,0:T(8,128)(2,1)}, u32[]{:S(2)}, u32[]{:S(2)}) collective-permute-start(bf16[1024,512]{1,0:T(8,128)(2,1)} %partial_keys.7), channel_id=1, source_target_pairs={{0,16},{16,0},{1,17},{17,1},{2,18},{18,2},{3,19},{19,3},{4,20},{20... | collective-permute-start | bytes 3145736 | tf_op jit(solution)/shard_map/ppermute | solution.py:318
  114.6 1.7 copy-start.3
  114.6 8.9 %copy-start.4 = (s32[1,3072]{1,0:T(1,128)S(1)}, s32[1,3072]{1,0:T(1,128)}, u32[]{:S(2)}) copy-start(s32[1,3072]{1,0:T(1,128)} %param.13) | copy-start | bytes 36868
  116.3 74.7 %all-to-all-start.2 = ((bf16[16,192,512]{2,1,0:T(8,128)(2,1)}), bf16[16,192,512]{2,1,0:T(8,128)(2,1)}, u32[]{:S(2)}, u32[]{:S(2)}) async-start(bf16[16,192,512]{2,1,0:T(8,128)(2,1)} %bitcast.18), calls=%async_computation.2 | async-start | bytes 6291456 | tf_op jit(solution)/shard_map/all_to_all | solution.py:309
